TPU v7x, 32 devices: a whole 2x2x4 slice. The times are simulated.
32 devices in a mesh: sec: 16 (over z, y, core), narrow: 2 (over x).
Axes of the slice: x: 2, y: 2, z: 4, core: 2. Of those that a mesh axis runs over, the one named last changes fastest.
Arguments:
- tokens: bfloat16 [2048, 2048], P('sec'), may hold values from -8 to 8
- attn_gain: float32 [2048], replicated, may hold values from 0.5 to 1.5
- w_query: bfloat16 [2048, 4096], P(None, 'narrow'), may hold values from -0.125 to 0.125
- w_key: bfloat16 [2048, 512], P(None, 'narrow'), may hold values from -0.125 to 0.125
- w_value: bfloat16 [2048, 512], P(None, 'narrow'), may hold values from -0.125 to 0.125
- query_gain: float32 [128], replicated, may hold values from 0.6 to 6
- key_gain: float32 [128], replicated, may hold values from 0.6 to 6
- w_out: bfloat16 [4096, 2048], P('narrow'), may hold values from -0.09375 to 0.09375
- moe_gain: float32 [2048], replicated, may hold values from 0.5 to 1.5
- expert_ids: int32 [2048, 8], P('sec'), may hold values from 0 to 63, all different within a row; in each aligned block of 64 rows (0 to 63, 64 to 127, ...) at most 20 rows name the same one
- expert_weights: float32 [2048, 8], P('sec'), may hold values from 0.05 to 1
- w_gate: bfloat16 [64, 2048, 768], P('sec', None, 'narrow'), may hold values from -0.125 to 0.125
- w_up: bfloat16 [64, 2048, 768], P('sec', None, 'narrow'), may hold values from -0.125 to 0.125
- w_down: bfloat16 [64, 768, 2048], P('sec', 'narrow'), may hold values from -0.21875 to 0.21875
Outputs:
- layer_out: bfloat16 [2048, 2048], P(('sec', 'narrow'))
Inputs may be any that keep to these rules, and one draw needn't show every extreme that they name: `expert_ids`: each row names 8 different experts. In each aligned block of 64 rows no expert is named by more than 20 rows, a bound that some block reaches.
All inputs are finite; a program needn't handle non-finite values.
Results may differ from a plain program's by a relative error of at most 0.009.
Values may be sent and summed in bfloat16 or wider, within the bound.
A program may use at most 128 MiB of HBM per device.

v0:
```python
import math

import jax
import jax.numpy as jnp
from jax import lax
from jax.sharding import PartitionSpec as P

D = 2048
HEADS = 32
KV_HEADS = 4
HEAD = 128
TOPK = 8


norm_eps = 1e-06


def rms_norm(inputs, gain):
    widened = inputs.astype(jnp.float32)
    return (
        widened * lax.rsqrt(jnp.mean(widened * widened, axis=-1, keepdims=True) + norm_eps) * gain
    )


def rotate(inputs, positions):
    half_size = inputs.shape[-1] // 2
    inverse = jnp.exp(
        -jnp.log(1000000.0) * jnp.arange(half_size, dtype=jnp.float32) * 2.0 / inputs.shape[-1]
    )
    angles = positions.astype(jnp.float32)[:, None] * inverse[None, :]
    cosine = jnp.cos(angles)[:, None, :]
    sine = jnp.sin(angles)[:, None, :]
    leading = inputs[..., :half_size]
    trailing = inputs[..., half_size:]
    return jnp.concatenate(
        [leading * cosine - trailing * sine, trailing * cosine + leading * sine], axis=-1
    )


def slot_numbers(flat_ids, experts_all):
    onehot = (
        flat_ids[:, :, None] == jnp.arange(experts_all, dtype=jnp.int32)[None, None, :]
    ).astype(jnp.int32)
    earlier = jnp.cumsum(onehot, axis=1) - onehot
    return jnp.sum(earlier * onehot, axis=-1)


def head_columns(whole, kv_start, kv_here):
    width = whole.shape[0]
    strided = whole.reshape(width, HEAD, KV_HEADS)
    picked = lax.dynamic_slice_in_dim(strided, kv_start, kv_here, 2)
    return jnp.transpose(picked, (0, 2, 1)).reshape(width, kv_here * HEAD)


def on_device(
    tokens,
    attn_gain,
    w_query,
    w_key,
    w_value,
    query_gain,
    key_gain,
    w_out,
    moe_gain,
    expert_ids,
    expert_weights,
    w_gate,
    w_up,
    w_down,
):
    sec_count = lax.axis_size("sec")
    narrow_count = lax.axis_size("narrow")
    sec_index = lax.axis_index("sec")
    narrow_index = lax.axis_index("narrow")
    local_rows = tokens.shape[0]
    share_rows = local_rows // narrow_count
    expert_here = w_gate.shape[0]
    experts_all = expert_here * sec_count
    capacity = min(share_rows, max(2, 5 * share_rows * TOPK // (2 * experts_all)))
    heads_here = w_query.shape[1] // HEAD
    group_size = HEADS // KV_HEADS
    kv_here = max(1, heads_here // group_size)
    per_key_head = heads_here // kv_here
    kv_start = narrow_index * heads_here // group_size
    scale = 1.0 / math.sqrt(HEAD)
    positions = sec_index * local_rows + jnp.arange(local_rows, dtype=jnp.int32)
    last_position = sec_index * local_rows + local_rows - 1
    normed = rms_norm(tokens, attn_gain).astype(jnp.bfloat16)
    query = jnp.dot(normed, w_query, preferred_element_type=jnp.float32).reshape(
        local_rows, heads_here, HEAD
    )
    query = rotate(rms_norm(query, query_gain), positions).astype(jnp.bfloat16)
    key_whole, value_whole = (
        lax.all_gather(w_key, "narrow", axis=1, tiled=True),
        lax.all_gather(w_value, "narrow", axis=1, tiled=True),
    )
    key_columns = head_columns(key_whole, kv_start, kv_here)
    value_columns = head_columns(value_whole, kv_start, kv_here)
    keys = jnp.dot(normed, key_columns, preferred_element_type=jnp.float32).reshape(
        local_rows, kv_here, HEAD
    )
    keys = (
        rotate(rms_norm(keys, key_gain), positions)
        .astype(jnp.bfloat16)
        .reshape(local_rows, kv_here * HEAD)
    )
    values = jnp.dot(normed, value_columns, preferred_element_type=jnp.float32).astype(jnp.bfloat16)
    grouped = query.reshape(local_rows, kv_here, per_key_head, HEAD)

    def update(state, block_keys, block_values, block_start):
        peak, total, accum = state
        width = block_keys.shape[0]
        scores = (
            jnp.einsum("tcgd,jcd->cgtj", grouped, block_keys, preferred_element_type=jnp.float32)
            * scale
        )
        key_positions = block_start + jnp.arange(width, dtype=jnp.int32)
        allowed = key_positions[None, :] <= positions[:, None]
        scores = jnp.where(allowed, scores, -1e30)
        new_peak = jnp.maximum(peak, jnp.max(scores, axis=-1))
        probs = jnp.where(allowed, jnp.exp(scores - new_peak[..., None]), 0.0)
        factor = jnp.exp(peak - new_peak)
        total = total * factor + jnp.sum(probs, axis=-1)
        accum = accum * factor[..., None] + jnp.einsum(
            "cgtj,jcd->cgtd",
            probs.astype(jnp.bfloat16),
            block_values,
            preferred_element_type=jnp.float32,
        )
        return (new_peak, total, accum)

    start_state = (
        jnp.full((kv_here, per_key_head, local_rows), -1e30, jnp.float32),
        jnp.zeros((kv_here, per_key_head, local_rows), jnp.float32),
        jnp.zeros((kv_here, per_key_head, local_rows, HEAD), jnp.float32),
    )
    carry = start_state
    key_piece = lax.all_gather(keys, "sec", axis=0, tiled=True)
    value_piece = lax.all_gather(values, "sec", axis=0, tiled=True)
    length = key_piece.shape[0]
    width = math.gcd(length, 512)
    blocks = length // width
    key_blocks = key_piece.reshape(blocks, width, kv_here, HEAD)
    value_blocks = value_piece.reshape(blocks, width, kv_here, HEAD)

    def advance(state, inputs):
        block_keys, block_values, number = inputs
        block_start = number * width
        state = lax.cond(
            block_start <= last_position,
            lambda inner: update(inner, block_keys, block_values, block_start),
            lambda inner: inner,
            state,
        )
        return (state, None)

    carry, _ = lax.scan(
        advance, carry, (key_blocks, value_blocks, jnp.arange(blocks, dtype=jnp.int32))
    )
    peak, total, accum = carry
    attended = (
        jnp.transpose(accum / total[..., None], (2, 0, 1, 3))
        .reshape(local_rows, heads_here * HEAD)
        .astype(jnp.bfloat16)
    )
    own_offset = narrow_index * share_rows
    mixed = lax.psum(
        jnp.dot(attended, w_out, preferred_element_type=jnp.float32).astype(jnp.bfloat16), "narrow"
    ).astype(jnp.float32)
    carried_all = (tokens.astype(jnp.float32) + mixed).astype(jnp.bfloat16)
    carried_mine = lax.dynamic_slice_in_dim(carried_all, own_offset, share_rows, 0)
    send_rows = rms_norm(carried_all, moe_gain).astype(jnp.bfloat16)

    def place(flat_ids, slots):
        return (flat_ids % expert_here * sec_count + flat_ids // expert_here) * capacity + slots

    out_rows = expert_here * sec_count * capacity
    flat_ids = expert_ids.reshape(narrow_count, share_rows * TOPK)
    slots = slot_numbers(flat_ids, experts_all)
    block_index = jnp.arange(narrow_count, dtype=jnp.int32)[:, None]
    targets = block_index * out_rows + place(flat_ids, slots)
    sources = (
        block_index * share_rows + jnp.arange(share_rows * TOPK, dtype=jnp.int32)[None, :] // TOPK
    )
    table = (
        jnp.full((narrow_count * out_rows,), narrow_count * share_rows, jnp.int32)
        .at[targets.reshape(-1)]
        .set(sources.reshape(-1))
    )
    padded = jnp.concatenate([send_rows, jnp.zeros((1, D), jnp.bfloat16)], axis=0)
    outgoing = padded[table].reshape(narrow_count, expert_here, sec_count, capacity, D)
    arrived = lax.all_to_all(outgoing, "sec", split_axis=2, concat_axis=2, tiled=True)
    count = arrived.shape[0]
    rows_in = arrived.reshape(count, expert_here, sec_count * capacity, D)
    gate_value = jnp.einsum("berd,edf->berf", rows_in, w_gate, preferred_element_type=jnp.float32)
    up_value = jnp.einsum("berd,edf->berf", rows_in, w_up, preferred_element_type=jnp.float32)
    active = (jax.nn.silu(gate_value) * up_value).astype(jnp.bfloat16)
    number = out_rows * lax.axis_size("narrow") // out_rows
    expert_total = lax.psum_scatter(
        jnp.einsum("berf,efd->berd", active, w_down, preferred_element_type=jnp.float32)
        .reshape(out_rows * lax.axis_size("narrow"), D)
        .astype(jnp.bfloat16),
        "narrow",
        scatter_dimension=0,
        tiled=True,
    )
    returned = lax.all_to_all(
        expert_total.reshape(1, expert_here, sec_count, capacity, D),
        "sec",
        split_axis=2,
        concat_axis=2,
        tiled=True,
    ).reshape(out_rows, D)
    own_ids = lax.dynamic_slice_in_dim(expert_ids, own_offset, share_rows, 0).reshape(
        1, share_rows * TOPK
    )
    own_slots = slot_numbers(own_ids, experts_all)
    picks = place(own_ids, own_slots).reshape(-1)
    gathered = returned[picks].reshape(share_rows, TOPK, D)
    own_weights = lax.dynamic_slice_in_dim(expert_weights, own_offset, share_rows, 0)
    gates = own_weights / jnp.sum(own_weights, axis=-1, keepdims=True)
    mixture = jnp.sum(gates[:, :, None] * gathered.astype(jnp.float32), axis=1)
    return (carried_mine.astype(jnp.float32) + mixture).astype(jnp.bfloat16)


def solution(mesh):
    in_specs = (
        P("sec", None),
        P(),
        P(None, "narrow"),
        P(None, "narrow"),
        P(None, "narrow"),
        P(),
        P(),
        P("narrow", None),
        P(),
        P("sec", None),
        P("sec", None),
        P("sec", None, "narrow"),
        P("sec", None, "narrow"),
        P("sec", "narrow", None),
    )
    out_specs = P(("sec", "narrow"), None)
    return jax.shard_map(
        on_device, mesh=mesh, in_specs=in_specs, out_specs=out_specs, check_vma=False
    )
```

profile of v0, /device:TPU:13, one launch (start us, length us, event | category | flops | bytes accessed | tf_op | source)
XLA Modules:
  0.0 868.6 jit_solution(1730297767140463340)
XLA Ops:
  9.5 33.6 %all-gather.5.cloned.1.call-done = bf16[2048,512]{1,0:T(8,128)(2,1)} async-done(((bf16[2048,256]{1,0:T(8,128)(2,1)}), bf16[2048,512]{1,0:T(8,128)(2,1)}) %all-gather.5.cloned.1.call-update) | async-done | bytes 2097168 | tf_op jit(solution)/shard_map/all_gather | solution.py:94
  43.1 2.9 copy.138
  48.3 29.5 %all-gather.9.cloned.1.call-done = bf16[2048,512]{1,0:T(8,128)(2,1)} async-done(((bf16[2048,256]{1,0:T(8,128)(2,1)}), bf16[2048,512]{1,0:T(8,128)(2,1)}) %all-gather.9.cloned.1.call-update) | async-done | bytes 2097168 | tf_op jit(solution)/shard_map/all_gather | solution.py:95
  77.8 2.9 copy.147
  83.0 4.5 dynamic-slice_bitcast_fusion
  89.3 4.7 convolution_bitcast_fusion
  101.7 24.9 %all-gather.7.cloned.1.call-done = bf16[2048,256]{1,0:T(8,128)(2,1)} async-done(((bf16[128,256]{1,0:T(8,128)(2,1)}), bf16[2048,256]{1,0:T(8,128)(2,1)}) %all-gather.7.cloned.1.call-update) | async-done | bytes 1048592 | tf_op jit(solution)/shard_map/all_gather | solution.py:138
  130.1 35.4 %all-gather.11.cloned.1.call-done = bf16[2048,256]{1,0:T(8,128)(2,1)} async-done(((bf16[128,256]{1,0:T(8,128)(2,1)}), bf16[2048,256]{1,0:T(8,128)(2,1)}) %all-gather.11.cloned.1.call-update) | async-done | bytes 1048592 | tf_op jit(solution)/shard_map/all_gather | solution.py:139
  171.2 16.4 %while.15 = (s32[]{:T(128)}, f32[2,8,128]{2,1,0:T(8,128)S(1)}, f32[2,8,128]{2,1,0:T(8,128)S(1)}, f32[2,8,128,128]{3,2,1,0:T(8,128)}, s32[4]{0:T(128)S(1)}, /*ind...) while((s32[]{:T(128)}, f32[2,8,128]{2,1,0:T(8,128)S(1)}, ...), condition=%wide.region_8.9_spmd.clone, body=%wide.region_3.8_spmd.clone.sunk | while | flops 551096960 | bytes 24517480 | solution.py:157
  172.4 5.7 conditional.3
  174.4 2.6 fusion.8
  179.3 5.7 conditional.3
  189.3 5.5 convolution_convert_fusion
  194.9 4.3 scatter_custom_fusion
  199.3 35.3 %all-reduce.3.cloned.1.call-done = bf16[128,2048]{1,0:T(8,128)(2,1)} async-done(((bf16[128,2048]{1,0:T(8,128)(2,1)}), bf16[128,2048]{1,0:T(8,128)(2,1)}) %all-reduce.3.cloned.1.call-update) | async-done | bytes 524304 | tf_op jit(solution)/shard_map/psum | solution.py:167
  236.2 10.9 %gather_fusion = bf16[2560,2048]{1,0:T(8,128)(2,1)} fusion(bf16[129,2048]{1,0:T(8,128)(2,1)S(1)} %concatenate.20, s32[3072]{0:T(1024)S(1)} %pad_clamp_fusion), kind=kCustom, calls=%fused_computation | custom fusion | bytes 20981760 | tf_op jit(solution)/shard_map/gather | solution.py:191
  247.0 16.4 %reshape.660 = bf16[2,4,16,20,2048]{4,3,2,1,0:T(8,128)(2,1)} reshape(bf16[2560,2048]{1,0:T(8,128)(2,1)} %gather_fusion) | data formatting | bytes 20971520 | tf_op jit(solution)/shard_map/reshape | solution.py:191
  263.4 12.5 %copy.157 = bf16[2,4,16,20,2048]{4,1,3,0,2:T(4,128)(2,1)S(1)} copy(bf16[2,4,16,20,2048]{4,3,2,1,0:T(8,128)(2,1)} %reshape.660) | data formatting | bytes 20971520 | tf_op jit(solution)/shard_map/reshape | solution.py:191
  275.9 233.5 %all_to_all.10 = bf16[2,4,16,20,2048]{4,1,3,0,2:T(4,128)(2,1)S(1)} all-to-all(bf16[2,4,16,20,2048]{4,1,3,0,2:T(4,128)(2,1)S(1)} %copy.157), channel_id=1, replica_groups=mesh['sec'=16,'narrow'=2] {'sec'}, dimensions={2} | all-to-all | bytes 20971520 | tf_op jit(solution)/shard_map/all_to_all | solution.py:192
  509.4 5.7 copy.158
  515.2 3.8 copy-done
  519.0 13.2 %fusion.21 = f32[4,2,320,384]{3,2,1,0:T(8,128)} fusion(bf16[2,4,320,2048]{3,1,2,0:T(4,128)(2,1)S(1)} %bitcast.166, bf16[4,2048,384]{2,1,0:T(8,128)(2,1)S(1)} %bitcast.186), kind=kOutput, calls=%fused_computation.28 | convolution fusion | flops 4026531840 | bytes 20709376 | tf_op jit(solution)/shard_map/berd,edf->berf/dot_general | solution.py:196
  532.2 30.4 %convert_bitcast_fusion = bf16[2,4,320,2048]{3,2,0,1:T(8,128)(2,1)} fusion(bf16[4,384,2048]{2,1,0:T(8,128)(2,1)} %param.31, f32[4,2,320,384]{3,2,1,0:T(8,128)} %fusion.21, bf16[4,2048,384]{2,1,0:T(8,128)(2,1)} %param.29, bf16[2,4,320,2048]{3,1,2,0:T(4,128)(2,1)} %bitcast.167), kind=kOutput, calls=%fused_computation.27 | convolution fusion | flops 8064204800 | bytes 37486592 | tf_op jit(solution)/shard_map/berf,efd->berd/dot_general | solution.py:200
  562.6 10.0 %copy.161 = bf16[2,4,320,2048]{3,2,1,0:T(8,128)(2,1)} copy(bf16[2,4,320,2048]{3,2,0,1:T(8,128)(2,1)} %convert_bitcast_fusion) | data formatting | bytes 20971520 | tf_op jit(solution)/shard_map/convert_element_type | solution.py:202
  572.7 121.6 %reduce-scatter.2.cloned.1.call-done = bf16[1280,2048]{1,0:T(8,128)(2,1)} async-done(((bf16[2560,2048]{1,0:T(8,128)(2,1)}), bf16[1280,2048]{1,0:T(8,128)(2,1)}) %reduce-scatter.2.cloned.1.call-update) | async-done | bytes 5242896 | tf_op jit(solution)/shard_map/reduce_scatter | solution.py:199
  694.2 9.1 %reshape.662 = bf16[1,4,16,20,2048]{4,3,2,1,0:T(8,128)(2,1)} reshape(bf16[1280,2048]{1,0:T(8,128)(2,1)} %reduce-scatter.2.cloned.1.call-done) | data formatting | bytes 10485760 | tf_op jit(solution)/shard_map/reshape | solution.py:208
  703.4 9.5 %copy.162 = bf16[1,4,16,20,2048]{4,1,3,0,2:T(4,128)(2,1)} copy(bf16[1,4,16,20,2048]{4,3,2,1,0:T(8,128)(2,1)} %reshape.662) | data formatting | bytes 10485760 | tf_op jit(solution)/shard_map/reshape | solution.py:208
  712.9 6.5 all-to-all-start.1
  722.2 112.1 %all-to-all-done.1 = bf16[1,4,16,20,2048]{4,1,3,0,2:T(4,128)(2,1)} async-done(((bf16[1,4,16,20,2048]{4,1,3,0,2:T(4,128)(2,1)}), bf16[1,4,16,20,2048]{4,1,3,0,2:T(4,128)(2,1)}, u32[]{:S(2)}, u32[]{:S(2)}) %all-to-all-start.1) | async-done | bytes 5242912 | tf_op jit(solution)/shard_map/all_to_all | solution.py:207
  834.3 8.1 copy.163
  842.4 9.0 %reshape.663 = bf16[1280,2048]{1,0:T(8,128)(2,1)} reshape(bf16[1,4,16,20,2048]{4,3,2,1,0:T(8,128)(2,1)} %copy.163) | data formatting | bytes 10485760 | tf_op jit(solution)/shard_map/reshape | solution.py:213
  851.4 7.6 gather_fusion.1
  (150 shorter events, 45.6 us)
Async XLA Ops:
  6.5 36.6 %all-gather.5.cloned.1.call-start = ((), (), s32[]{:S(2)}) async-start(), calls=%async_computation.3 | async-start | bytes 3145728 | tf_op jit(solution)/shard_map/all_gather | solution.py:94
  7.3 70.5 %all-gather.9.cloned.1.call-start = ((), (), s32[]{:S(2)}) async-start(), calls=%async_computation.5 | async-start | bytes 3145728 | tf_op jit(solution)/shard_map/all_gather | solution.py:95
  8.0 118.5 %all-gather.7.cloned.1.call-start = ((), (), s32[]{:S(2)}) async-start(), calls=%async_computation.4 | async-start | bytes 1114112 | tf_op jit(solution)/shard_map/all_gather | solution.py:138
  80.7 6.7 copy-start.1
  80.7 6.7 copy-start.4
  83.0 5.3 copy-start.8
  89.2 76.2 %all-gather.11.cloned.1.call-start = ((), (), s32[]{:S(2)}) async-start(), calls=%async_computation.6 | async-start | bytes 1114112 | tf_op jit(solution)/shard_map/all_gather | solution.py:139
  94.0 2.6 copy-start.5
  94.0 3.1 copy-start.9
  96.1 138.5 %all-reduce.3.cloned.1.call-start = ((), (), s32[]{:S(2)}) async-start(), calls=%async_computation.7 | async-start | bytes 1048576 | tf_op jit(solution)/shard_map/psum | solution.py:167
  172.6 1.8 copy-start.2
  177.1 1.0 copy-start.3
  179.5 1.8 copy-start.2
  184.0 1.0 copy-start.3
  189.3 46.6 %copy-start.7 = (f32[2048]{0:T(1024)S(1)}, f32[2048]{0:T(1024)}, u32[]{:S(2)}) copy-start(f32[2048]{0:T(1024)} %param.26) | copy-start | bytes 24580
  194.8 499.4 %reduce-scatter.2.cloned.1.call-start = ((), (), s32[]{:S(2)}) async-start(), calls=%async_computation.8 | async-start | bytes 15728640 | tf_op jit(solution)/shard_map/reduce_scatter | solution.py:199
  275.9 243.1 %slice-start = ((s8[6291456]{0:T(1024)(128)(4,1)}), s8[4194304]{0:T(1024)(128)(4,1)S(1)}, s32[]{:S(2)}) async-start(s8[6291456]{0:T(1024)(128)(4,1)} %bitcast.185), calls=%async_computation.9 | async-start | bytes 8388608
  509.4 9.6 %slice-start.1 = ((s8[6291456]{0:T(1024)(128)(4,1)}), s8[2097152]{0:T(1024)(128)(4,1)S(1)}, s32[]{:S(2)}) async-start(s8[6291456]{0:T(1024)(128)(4,1)} %bitcast.185), calls=%async_computation.10 | async-start | bytes 4194304
  515.2 3.8 copy-start
  712.9 8.6 copy-start.6
  712.9 121.4 %all-to-all-start.1 = ((bf16[1,4,16,20,2048]{4,1,3,0,2:T(4,128)(2,1)}), bf16[1,4,16,20,2048]{4,1,3,0,2:T(4,128)(2,1)}, u32[]{:S(2)}, u32[]{:S(2)}) async-start(bf16[1,4,16,20,2048]{4,1,3,0,2:T(4,128)(2,1)} %copy.162), calls=%async_computation.2 | async-start | bytes 10485760 | tf_op jit(solution)/shard_map/all_to_all | solution.py:207
Sparse Core Ops, SparseCore 0:
  8.9 34.1 all-gather.4
  44.7 33.0 all-gather.8
  89.3 37.1 all-gather.6
  128.6 36.8 all-gather.10
  194.9 39.6 all-reduce.2
  572.8 121.3 reduce-scatter.1
where the time goes:
time: 876 us; the launch traced here: 869 us
  waiting for transfers between devices  394 us (45%)
  blocking collectives  234 us (27%)
  local copies, waits for them, and re-layouts  141 us (16%)
  matrix products  62.5 us (7%)
  other arithmetic  14.2 us (2%)
  between operations  14.2 us (2%)
    all_to_all x1, blocking collectives, on_device(): lax.all_to_all(outgoing, 'sec', split_axis=2, concat_axis=2, tiled=True)  234 us
    reduce_scatter x1, waiting for transfers between devices, on_device(): lax.psum_scatter(jnp.einsum('berf,efd->berd', active, w_down, preferred_e...  122 us
    all_to_all x1, waiting for transfers between devices, on_device(): lax.all_to_all(expert_total.reshape(1, expert_here, sec_count, capacity,...  112 us
    all_gather x1, waiting for transfers between devices, on_device(): value_piece = lax.all_gather(values, 'sec', axis=0, tiled=True)  35.4 us
    psum x1, waiting for transfers between devices, on_device(): lax.psum(jnp.dot(attended, w_out, preferred_element_type=jnp.float32).ast...  35.3 us
    all_gather x1, waiting for transfers between devices, on_device(): lax.all_gather(w_key, 'narrow', axis=1, tiled=True)  33.6 us
    dot_general x1, matrix products, on_device(): jnp.einsum('berf,efd->berd', active, w_down, preferred_element_type=jnp.f...  30.4 us
    all_gather x1, waiting for transfers between devices, on_device(): lax.all_gather(w_value, 'narrow', axis=1, tiled=True)  29.5 us
  transfers between devices with their start and end apart: 7, of which 7 were waited for; matrix products, arithmetic and copies ran while one was open for 3% of the time, Pallas kernels for 0%

commit v1 on v0

v1 whole, which is shorter than its diff:
```python
import functools
import math

import jax
import jax.numpy as jnp
from jax import lax
from jax.experimental import pallas as pl
from jax.experimental.pallas import tpu as pltpu
from jax.sharding import PartitionSpec as P

D = 2048
HEADS = 32
KV_HEADS = 4
HEAD = 128
TOPK = 8


norm_eps = 1e-06


def rms_norm(inputs, gain):
    widened = inputs.astype(jnp.float32)
    return (
        widened * lax.rsqrt(jnp.mean(widened * widened, axis=-1, keepdims=True) + norm_eps) * gain
    )


def rotate(inputs, positions):
    half_size = inputs.shape[-1] // 2
    inverse = jnp.exp(
        -jnp.log(1000000.0) * jnp.arange(half_size, dtype=jnp.float32) * 2.0 / inputs.shape[-1]
    )
    angles = positions.astype(jnp.float32)[:, None] * inverse[None, :]
    cosine = jnp.cos(angles)[:, None, :]
    sine = jnp.sin(angles)[:, None, :]
    leading = inputs[..., :half_size]
    trailing = inputs[..., half_size:]
    return jnp.concatenate(
        [leading * cosine - trailing * sine, trailing * cosine + leading * sine], axis=-1
    )


VMEM_LIMIT = 60 * 1024 * 1024


def whole(shape):
    zeros = (0,) * len(shape)
    return pl.BlockSpec(shape, lambda *_: zeros, pipeline_mode=pl.Buffered(1))


def attention_kernel(width, local_rows, q_ref, k_ref, v_ref, o_ref):
    first = lax.axis_index("sec") * local_rows
    rows = q_ref.shape[0]
    q = q_ref[...]
    factor = math.log2(math.e) / math.sqrt(HEAD)
    positions = first + lax.rem(lax.broadcasted_iota(jnp.int32, (rows, width), 0), local_rows)
    columns = lax.broadcasted_iota(jnp.int32, (rows, width), 1)

    def advance(number, state):
        peak, total, accum = state
        start = pl.multiple_of(number * width, width)
        scores = lax.dot_general(
            q, k_ref[pl.ds(start, width), :], (((1,), (1,)), ((), ())),
            preferred_element_type=jnp.float32,
        ) * factor
        scores = jnp.where(columns + start <= positions, scores, -1e30)
        new_peak = jnp.maximum(peak, jnp.max(scores, axis=-1, keepdims=True))
        probs = jnp.exp2(scores - new_peak)
        shrink = jnp.exp2(peak - new_peak)
        total = total * shrink + jnp.sum(probs, axis=-1, keepdims=True)
        accum = accum * shrink + jnp.dot(
            probs.astype(jnp.bfloat16), v_ref[pl.ds(start, width), :],
            preferred_element_type=jnp.float32,
        )
        return new_peak, total, accum

    blocks = (first + local_rows - 1) // width + 1
    _, total, accum = lax.fori_loop(
        0,
        blocks,
        advance,
        (
            jnp.full((rows, 1), -1e30, jnp.float32),
            jnp.zeros((rows, 1), jnp.float32),
            jnp.zeros((rows, HEAD), jnp.float32),
        ),
    )
    o_ref[...] = (accum / total).astype(jnp.bfloat16)


def attention(query, keys_values, kv_here, per_key_head, local_rows):
    length = keys_values.shape[0]
    width = math.gcd(length, 512)
    together = math.gcd(per_key_head, 2)
    steps = per_key_head // together
    tall = together * local_rows
    return pl.pallas_call(
        functools.partial(attention_kernel, width, local_rows),
        grid=(kv_here, steps),
        in_specs=[
            pl.BlockSpec((tall, HEAD), lambda c, s: (c * steps + s, 0)),
            pl.BlockSpec((length, HEAD), lambda c, s: (0, c)),
            pl.BlockSpec((length, HEAD), lambda c, s: (0, kv_here + c)),
        ],
        out_specs=pl.BlockSpec((tall, HEAD), lambda c, s: (c * steps + s, 0)),
        out_shape=jax.ShapeDtypeStruct(query.shape, jnp.bfloat16),
        compiler_params=pltpu.CompilerParams(vmem_limit_bytes=VMEM_LIMIT),
    )(query, keys_values, keys_values)


def experts_kernel(x_ref, pick_ref, back_ref, weight_ref, gate_ref, up_ref, down_ref, o_ref, rows_ref, y_ref):
    step = pl.program_id(0)
    blocks, slots, block_rows = pick_ref.shape[1:]
    experts = y_ref.shape[0]
    for b in range(blocks):
        rows_ref[b * slots : (b + 1) * slots, :] = jnp.dot(
            pick_ref[0, b], x_ref[b * block_rows : (b + 1) * block_rows, :],
            preferred_element_type=jnp.float32,
        ).astype(jnp.bfloat16)
    rows = rows_ref[...]
    gate = jnp.dot(rows, gate_ref[0], preferred_element_type=jnp.float32)
    up = jnp.dot(rows, up_ref[0], preferred_element_type=jnp.float32)
    active = (gate / (1.0 + jnp.exp(-gate)) * up).astype(jnp.bfloat16)
    tile = math.gcd(o_ref.shape[1], 512)
    for c in range(0, o_ref.shape[1], tile):
        y_ref[step, :, c : c + tile] = (
            jnp.dot(active, down_ref[0, :, c : c + tile], preferred_element_type=jnp.float32)
            * weight_ref[0]
        ).astype(jnp.bfloat16)

    @pl.when(step == experts - 1)
    def _():
        for b in range(blocks):
            total = jnp.zeros((block_rows, o_ref.shape[1]), jnp.float32)
            for e in range(experts):
                total += jnp.dot(
                    back_ref[e, b], y_ref[e, b * slots : (b + 1) * slots, :],
                    preferred_element_type=jnp.float32,
                )
            o_ref[b * block_rows : (b + 1) * block_rows, :] = total.astype(jnp.bfloat16)


def experts_local(x, ids, gates, capacity, w_gate, w_up, w_down, first_expert):
    rows_all = x.shape[0]
    block_rows, slots = capacity
    experts = w_gate.shape[0]
    hidden = w_gate.shape[2]
    blocks = rows_all // block_rows
    mine = ids[:, :, None] == first_expert + jnp.arange(experts, dtype=jnp.int32)[None, None, :]
    hit = jnp.any(mine, axis=1)
    weight = jnp.sum(jnp.where(mine, gates[:, :, None], 0.0), axis=1)
    hit_blocks = hit.reshape(blocks, block_rows, experts).transpose(2, 0, 1)
    weight_blocks = weight.reshape(blocks, block_rows, experts).transpose(2, 0, 1)
    order = jnp.arange(block_rows, dtype=jnp.int32)
    before = (order[:, None] < order[None, :]).astype(jnp.bfloat16)
    rank = jnp.dot(
        hit_blocks.astype(jnp.bfloat16).reshape(experts * blocks, block_rows), before,
        preferred_element_type=jnp.float32,
    ).reshape(experts, blocks, block_rows).astype(jnp.int32)
    rank = jnp.where(hit_blocks, rank, -1)
    number = jnp.arange(slots, dtype=jnp.int32)
    taken = rank[:, :, None, :] == number[None, None, :, None]
    pick = taken.astype(jnp.bfloat16)
    back = (rank[:, :, :, None] == number[None, None, None, :]).astype(jnp.bfloat16)
    slot_weight = jnp.sum(
        jnp.where(taken, weight_blocks[:, :, None, :], 0.0), axis=-1
    ).reshape(experts, blocks * slots, 1)
    total = blocks * slots
    return pl.pallas_call(
        experts_kernel,
        grid=(experts,),
        in_specs=[
            whole(x.shape),
            pl.BlockSpec((1, blocks, slots, block_rows), lambda e: (e, 0, 0, 0)),
            whole(back.shape),
            pl.BlockSpec((1, total, 1), lambda e: (e, 0, 0)),
            pl.BlockSpec((1, D, hidden), lambda e: (e, 0, 0)),
            pl.BlockSpec((1, D, hidden), lambda e: (e, 0, 0)),
            pl.BlockSpec((1, hidden, D), lambda e: (e, 0, 0)),
        ],
        out_specs=whole(x.shape),
        out_shape=jax.ShapeDtypeStruct(x.shape, jnp.bfloat16),
        scratch_shapes=[
            pltpu.VMEM((total, D), jnp.bfloat16),
            pltpu.VMEM((experts, total, D), jnp.bfloat16),
        ],
        compiler_params=pltpu.CompilerParams(vmem_limit_bytes=VMEM_LIMIT),
    )(x, pick, back, slot_weight, w_gate, w_up, w_down)


def exchange(pieces_for, count, index, axis):
    own = pieces_for(index)
    held = jnp.zeros((count,) + own.shape, own.dtype)
    held = lax.dynamic_update_slice_in_dim(held, own[None], index, 0)
    for shift in range(1, count):
        target = lax.rem(index + shift, count)
        source = lax.rem(index + count - shift, count)
        piece = lax.ppermute(
            pieces_for(target), axis, [(i, (i + shift) % count) for i in range(count)]
        )
        held = lax.dynamic_update_slice_in_dim(held, piece[None], source, 0)
    return held


def on_device(
    tokens, attn_gain, w_query, w_key, w_value, query_gain, key_gain, w_out, moe_gain,
    expert_ids, expert_weights, w_gate, w_up, w_down,
):
    sec_count = lax.axis_size("sec")
    narrow_count = lax.axis_size("narrow")
    sec_index = lax.axis_index("sec")
    narrow_index = lax.axis_index("narrow")
    local_rows = tokens.shape[0]
    share_rows = local_rows // narrow_count
    expert_here = w_gate.shape[0]
    experts_all = expert_here * sec_count
    capacity = min(share_rows, max(2, 5 * share_rows * TOPK // (2 * experts_all)))
    heads_here = w_query.shape[1] // HEAD
    group_size = HEADS // KV_HEADS
    kv_here = max(1, heads_here // group_size)
    per_key_head = heads_here // kv_here
    part = HEAD // narrow_count
    positions = sec_index * local_rows + jnp.arange(local_rows, dtype=jnp.int32)
    normed = rms_norm(tokens, attn_gain).astype(jnp.bfloat16)

    columns = jnp.arange(w_key.shape[1], dtype=jnp.int32)
    sorted_at = columns % KV_HEADS * part + columns // KV_HEADS
    order = (sorted_at[:, None] == columns[None, :]).astype(jnp.bfloat16)
    both = jnp.concatenate(
        [
            jnp.dot(w, order, preferred_element_type=jnp.float32).astype(jnp.bfloat16)
            for w in (w_key, w_value)
        ],
        axis=1,
    )
    kv_part = jnp.dot(normed, both, preferred_element_type=jnp.float32)
    kv_part = kv_part.reshape(local_rows, 2, KV_HEADS * part)

    def for_peer(peer):
        start = peer * heads_here // group_size * part
        return lax.dynamic_slice_in_dim(kv_part, start, kv_here * part, 2)

    held = exchange(for_peer, narrow_count, narrow_index, "narrow")
    held = held.reshape(narrow_count, local_rows, 2, kv_here, part)
    held = jnp.transpose(held, (1, 2, 3, 0, 4)).reshape(local_rows, 2, kv_here, HEAD)
    keys = rotate(rms_norm(held[:, 0], key_gain), positions).astype(jnp.bfloat16)
    values = held[:, 1].astype(jnp.bfloat16)

    gates_own = expert_weights / jnp.sum(expert_weights, axis=-1, keepdims=True)
    keys_values = jnp.concatenate([keys, values], axis=1).reshape(local_rows, 2 * kv_here * HEAD)
    keys_values = lax.all_gather(keys_values, "sec", axis=0, tiled=True)
    routing = lax.all_gather(
        jnp.concatenate([expert_ids.astype(jnp.float32), gates_own], axis=1), "sec", axis=0,
        tiled=True,
    )
    ids = routing[:, :TOPK].astype(jnp.int32)
    gates = routing[:, TOPK:]

    query = jnp.dot(normed, w_query, preferred_element_type=jnp.float32).reshape(
        local_rows, heads_here, HEAD
    )
    query = rotate(rms_norm(query, query_gain), positions).astype(jnp.bfloat16)
    query = jnp.transpose(query, (1, 0, 2)).reshape(heads_here * local_rows, HEAD)
    attended = attention(query, keys_values, kv_here, per_key_head, local_rows)
    attended = jnp.transpose(
        attended.reshape(heads_here, local_rows, HEAD), (1, 0, 2)
    ).reshape(local_rows, heads_here * HEAD)

    own_offset = narrow_index * share_rows
    mixed = jnp.dot(attended, w_out, preferred_element_type=jnp.float32).astype(jnp.bfloat16)
    mixed = exchange(
        lambda peer: lax.dynamic_slice_in_dim(mixed, peer * share_rows, share_rows, 0),
        narrow_count, narrow_index, "narrow",
    )
    mixed = jnp.sum(mixed.astype(jnp.float32), axis=0)
    tokens_mine = lax.dynamic_slice_in_dim(tokens, own_offset, share_rows, 0)
    carried = (tokens_mine.astype(jnp.float32) + mixed).astype(jnp.bfloat16)
    moe_in = rms_norm(carried, moe_gain).astype(jnp.bfloat16)
    moe_all = lax.all_gather(moe_in, ("sec", "narrow"), axis=0, tiled=True)

    block_rows, slots = local_rows, narrow_count * capacity
    while slots % 16:
        block_rows, slots = 2 * block_rows, 2 * slots
    mixture = experts_local(
        moe_all, ids, gates, (block_rows, slots), w_gate, w_up, w_down, sec_index * expert_here
    )
    mixture = lax.psum_scatter(mixture, ("sec", "narrow"), scatter_dimension=0, tiled=True)
    return (carried.astype(jnp.float32) + mixture.astype(jnp.float32)).astype(jnp.bfloat16)


def solution(mesh):
    in_specs = (
        P("sec", None),
        P(),
        P(None, "narrow"),
        P(None, "narrow"),
        P(None, "narrow"),
        P(),
        P(),
        P("narrow", None),
        P(),
        P("sec", None),
        P("sec", None),
        P("sec", None, "narrow"),
        P("sec", None, "narrow"),
        P("sec", "narrow", None),
    )
    out_specs = P(("sec", "narrow"), None)
    return jax.shard_map(
        on_device, mesh=mesh, in_specs=in_specs, out_specs=out_specs, check_vma=False
    )
```

time: 876 us -> 404 us (0.46)
  blocking collectives: 234 us -> 24.9 us
  local copies, waits for them, and re-layouts: 141 us -> 6.36 us
  waiting for transfers between devices: 394 us -> 279 us
  Pallas kernels: 0 us -> 51.8 us
  matrix products: 62.5 us -> 11.5 us
    all_to_all x1 -> x0, blocking collectives: 234 us -> none  [on_device(): lax.all_to_all(outgoing, 'sec', split_axis=2, concat_axis=2, tiled=True)]
    all_to_all x1 -> x0, waiting for transfers between devices: 112 us -> none  [on_device(): lax.all_to_all(expert_total.reshape(1, expert_here, sec_count, capacity,...]
    reshape x11 -> x4, local copies, waits for them, and re-layouts: 65.5 us -> 3.91 us  [the longest x1 1.66 us: experts_local(): slot_weight = jnp.sum(jnp.where(taken, weight_blocks[:, :, None, :], 0.0)...]
    reduce_scatter x1, waiting for transfers between devices: 122 us -> 181 us  [on_device(): lax.psum_scatter(mixture, ('sec', 'narrow'), scatter_dimension=0, tiled=T...]
    pallas_call x0 -> x2, Pallas kernels: none -> 51.8 us  [the longest x1 41 us: experts_local(): pl.pallas_call(experts_kernel, grid=(experts,), in_specs=[whole(x.shape),...]
    dot_general x8 -> x4, matrix products: 52.4 us -> 2.13 us  [the longest x2 1.14 us: on_device(): jnp.dot(w, order, preferred_element_type=jnp.float32).astype(jnp.bfloat16)]
    psum x1 -> x0, waiting for transfers between devices: 35.3 us -> none  [on_device(): lax.psum(jnp.dot(attended, w_out, preferred_element_type=jnp.float32).ast...]
    all_gather x4 -> x2, waiting for transfers between devices: 123 us -> 89.1 us  [the longest x1 54.8 us: on_device(): moe_all = lax.all_gather(moe_in, ('sec', 'narrow'), axis=0, tiled=True)]
  transfers between devices with their start and end apart: 7 -> 5, of which waited for: 7 -> 5; matrix products, arithmetic and copies ran while one was open for 3% -> 4% of each run, Pallas kernels for 0% -> 0%
where the time goes in v1:
time: 404 us; the launch traced here: 401 us
  waiting for transfers between devices  279 us (69%)
  Pallas kernels  51.8 us (13%)
  blocking collectives  24.9 us (6%)
  between operations  13.6 us (3%)
  matrix products  11.5 us (3%)
  other arithmetic  11.3 us (3%)
  local copies, waits for them, and re-layouts  6.36 us (2%)
    reduce_scatter x1, waiting for transfers between devices, on_device(): lax.psum_scatter(mixture, ('sec', 'narrow'), scatter_dimension=0, tiled=T...  181 us
    all_gather x1, waiting for transfers between devices, on_device(): moe_all = lax.all_gather(moe_in, ('sec', 'narrow'), axis=0, tiled=True)  54.8 us
    pallas_call x1, Pallas kernels, experts_local(): pl.pallas_call(experts_kernel, grid=(experts,), in_specs=[whole(x.shape),...  41 us
    all_gather x1, waiting for transfers between devices, on_device(): keys_values = lax.all_gather(keys_values, 'sec', axis=0, tiled=True)  34.3 us
    all_gather x1, blocking collectives, on_device(): lax.all_gather(jnp.concatenate([expert_ids.astype(jnp.float32), gates_own...  24.9 us
    pallas_call x1, Pallas kernels, attention(): pl.pallas_call(functools.partial(attention_kernel, width, local_rows), gr...  10.7 us
    ppermute x2, waiting for transfers between devices, exchange(): lax.ppermute(pieces_for(target), axis, [(i, (i + shift) % count) for i in...  9.09 us
  transfers between devices with their start and end apart: 5, of which 5 were waited for; matrix products, arithmetic and copies ran while one was open for 4% of the time, Pallas kernels for 0%

profile of v1, /device:TPU:13, one launch (start us, length us, event | category | flops | bytes accessed | tf_op | source)
XLA Modules:
  0.0 401.5 jit_solution(16195892285004963306)
XLA Ops:
  6.6 1.4 fusion.9
  8.2 0.6 fusion.3
  8.8 0.6 fusion.2
  9.4 0.8 fusion.4
  10.5 0.3 constant_dynamic-slice_fusion.1
  10.9 1.3 collective-permute-start
  12.4 0.2 multiply_cosine_fusion
  12.6 2.7 collective-permute-done
  15.6 0.8 copy.60
  16.6 4.7 %convolution_bitcast_fusion = f32[16,8,16,128]{3,1,2,0:T(8,128)S(1)} fusion(bf16[2048,2048]{1,0:T(8,128)(2,1)} %param.16, bf16[128,2048]{1,0:T(8,128)(2,1)S(1)} %copy-done.2, f32[2048]{0:T(1024)S(1)} %copy-done.4, f32[128]{0:T(128)S(1)} %add_rsqrt_fusion.3), kind=kOutput, calls=%fused_computation.14 | convolution fusion | flops 1074790400 | bytes 9970176 | tf_op jit(solution)/shard_map/dot_general | solution.py:259
  21.5 0.3 multiply_reduce_fusion
  22.1 0.3 multiply_multiply_fusion
  22.4 0.5 subtract_convert_fusion
  23.0 0.3 maximum_bitcast_fusion
  23.3 0.9 copy.53
  24.2 34.3 %all-gather.3.cloned.1.call-done.k_ref.v_ref = bf16[2048,512]{1,0:T(8,128)(2,1)} async-done(((bf16[128,512]{1,0:T(8,128)(2,1)}), bf16[2048,512]{1,0:T(8,128)(2,1)}) %all-gather.3.cloned.1.call-update) | async-done | bytes 2097168 | tf_op jit(solution)/shard_map/all_gather | solution.py:251
  58.5 10.7 %shard_map.136 = bf16[2048,128]{1,0:T(8,128)(2,1)} custom-call(bf16[2048,128]{1,0:T(8,128)(2,1)} %bitcast.70, bf16[2048,512]{1,0:T(8,128)(2,1)} %all-gather.3.cloned.1.call-done.k_ref.v_ref, bf16[2048,512]{1,0:T(8,128)(2,1)} %all-gather.3.cloned.1.call-done.k_ref.v_ref), custom_call_target="tpu_custom_call" | custom-call | tf_op jit(solution)/shard_map/pallas_call | solution.py:97
  69.2 1.3 copy.58
  70.5 4.7 %convolution_convert_fusion.2 = bf16[128,2048]{1,0:T(8,128)(2,1)S(1)} fusion(bf16[128,2048]{0,1:T(8,128)(2,1)S(1)} %bitcast.69, bf16[2048,2048]{1,0:T(8,128)(2,1)} %param.21), kind=kOutput, calls=%fused_computation.9 | convolution fusion | flops 1074003968 | bytes 9437184 | tf_op jit(solution)/shard_map/dot_general | solution.py:270
  75.3 1.3 collective-permute-start.1
  76.6 6.4 %collective-permute-done.1 = bf16[64,2048]{1,0:T(8,128)(2,1)S(1)} collective-permute-done((bf16[64,2048]{1,0:T(8,128)(2,1)S(1)}, bf16[64,2048]{1,0:T(8,128)(2,1)S(1)}, u32[]{:S(2)}, u32[]{:S(2)}) %collective-permute-start.1) | collective-permute-done | bytes 262176 | tf_op jit(solution)/shard_map/ppermute | solution.py:198
  83.1 0.2 fusion.12
  83.3 0.8 fusion.14
  84.3 24.9 %all_gather.11 = f32[2048,16]{0,1:T(8,128)S(1)} all-gather(f32[128,16]{0,1:T(8,128)S(1)} %pad_maximum_fusion.1), channel_id=1, replica_groups=mesh['sec'=16,'narrow'=2] {'sec'}, dimensions={0}, use_global_device_ids=true | all-gather | bytes 139264 | tf_op jit(solution)/shard_map/all_gather | solution.py:252
  109.6 0.6 select_reduce_fusion
  110.3 1.7 reshape.176.weight_ref
  111.9 1.5 fusion.1.pick_ref
  113.5 2.7 fusion.back_ref
  116.1 54.8 %all-gather.5.cloned.1.call-done.x_ref = bf16[2048,2048]{1,0:T(8,128)(2,1)} async-done(((bf16[64,2048]{1,0:T(8,128)(2,1)}), bf16[2048,2048]{1,0:T(8,128)(2,1)}) %all-gather.5.cloned.1.call-update) | async-done | bytes 8388624 | tf_op jit(solution)/shard_map/all_gather | solution.py:279
  170.9 41.0 %shard_map.137 = bf16[2048,2048]{1,0:T(8,128)(2,1)} custom-call(bf16[2048,2048]{1,0:T(8,128)(2,1)} %all-gather.5.cloned.1.call-done.x_ref, bf16[4,8,80,256]{3,2,1,0:T(8,128)(2,1)} %fusion.1.pick_ref, bf16[4,8,256,80]{3,2,1,0:T(8,128)(2,1)} %fusion.back_ref, f32[4,640,1]{2,1,0:T(8,128)} %reshape.176.weight_ref, bf16[4,2048,384]{2,1,0:T(8,128)(2,1)} %gate_ref.1, ...), custom_call_target="tpu_custom_call" | custom-call | tf_op jit(solution)/shard_map/pallas_call | solution.py:169
  212.0 181.2 %reduce-scatter.2.cloned.1.call-done = bf16[64,2048]{1,0:T(8,128)(2,1)} async-done(((bf16[2048,2048]{1,0:T(8,128)(2,1)}), bf16[64,2048]{1,0:T(8,128)(2,1)}) %reduce-scatter.2.cloned.1.call-update) | async-done | bytes 262160 | tf_op jit(solution)/shard_map/reduce_scatter | solution.py:287
  393.2 1.7 fusion.15
  (65 shorter events, 2.3 us)
Async XLA Ops:
  6.5 1.7 copy-start
  6.5 2.9 copy-start.2
  6.5 2.3 copy-start.3
  6.5 2.9 copy-start.4
  6.5 51.9 %all-gather.3.cloned.1.call-start = ((), (), s32[]{:S(2)}) async-start(), calls=%async_computation.1 | async-start | bytes 2228224 | tf_op jit(solution)/shard_map/all_gather | solution.py:251
  10.3 5.2 %copy-start.8 = (f32[128]{0:T(128)S(1)}, f32[128]{0:T(128)}, u32[]{:S(2)}) copy-start(f32[128]{0:T(128)} %param.20) | copy-start | bytes 1540
  10.9 4.4 %collective-permute-start = (f32[128,2,128]{0,2,1:T(8,128)S(1)}, f32[128,2,128]{0,2,1:T(8,128)S(1)}, u32[]{:S(2)}, u32[]{:S(2)}) collective-permute-start(f32[128,2,128]{0,2,1:T(8,128)S(1)} %copy.61), channel_id=1, source_target_pairs={{0,1},{1,0},{2,3},{3,2},{4,5},{5,4},{6,7},{7,6},{8,9},{9,8},{10,11... | collective-permute-start | bytes 393224 | tf_op jit(solution)/shard_map/ppermute | solution.py:198
  16.4 154.5 %all-gather.5.cloned.1.call-start = ((), (), s32[]{:S(2)}) async-start(), calls=%async_computation.2 | async-start | bytes 8650752 | tf_op jit(solution)/shard_map/all_gather | solution.py:279
  21.3 0.7 copy-start.9
  75.2 8.1 %copy-start.6 = (f32[2048]{0:T(1024)S(1)}, f32[2048]{0:T(1024)}, u32[]{:S(2)}) copy-start(f32[2048]{0:T(1024)} %param.22) | copy-start | bytes 24580
  75.2 9.0 %copy-start.5 = (f32[128,8]{0,1:T(8,128)S(1)}, f32[128,8]{0,1:T(8,128)}, u32[]{:S(2)}) copy-start(f32[128,8]{0,1:T(8,128)} %param.24) | copy-start | bytes 12292
  75.2 9.0 %copy-start.7 = (s32[128,8]{0,1:T(8,128)S(1)}, s32[128,8]{0,1:T(8,128)}, u32[]{:S(2)}) copy-start(s32[128,8]{0,1:T(8,128)} %param.23) | copy-start | bytes 12292
  75.3 7.7 %collective-permute-start.1 = (bf16[64,2048]{1,0:T(8,128)(2,1)S(1)}, bf16[64,2048]{1,0:T(8,128)(2,1)S(1)}, u32[]{:S(2)}, u32[]{:S(2)}) collective-permute-start(bf16[64,2048]{1,0:T(8,128)(2,1)S(1)} %constant_dynamic-slice_fusion), channel_id=1, source_target_pairs={{0,1},{1,0},{2,3},{3,2},{4,5},{5,4},{6,7},{7,6},{8,9},{9,8},{10,11... | collective-permute-start | bytes 786440 | tf_op jit(solution)/shard_map/ppermute | solution.py:198
  84.2 309.1 %reduce-scatter.2.cloned.1.call-start = ((), (), s32[]{:S(2)}) async-start(), calls=%async_computation.3 | async-start | bytes 8650752 | tf_op jit(solution)/shard_map/reduce_scatter | solution.py:287
  211.9 183.0 %copy-start.1 = (bf16[2048,256]{1,0:T(8,128)(2,1)S(1)}, bf16[2048,256]{1,0:T(8,128)(2,1)}, u32[]{:S(2)}) copy-start(bf16[2048,256]{1,0:T(8,128)(2,1)} %param.18) | copy-start | bytes 3145732
Sparse Core Ops, SparseCore 0:
  16.5 41.9 all-gather.2
  84.3 86.5 all-gather.4
  212.1 181.0 reduce-scatter.1

commit v2 on v1

--- a/solution.py
+++ b/solution.py
@@ -202,6 +202,53 @@
     return held
 
 
+def swap_bit(piece, bit, count):
+    return lax.ppermute(piece, "sec", [(i, i ^ (1 << bit)) for i in range(count)])
+
+
+def halves_reduce(partial, orders, share_rows):
+    sec_count = lax.axis_size("sec")
+    narrow_count = lax.axis_size("narrow")
+    sec_index = lax.axis_index("sec")
+    narrow_index = lax.axis_index("narrow")
+    bits = sec_count.bit_length() - 1
+    wide = partial.shape[1] // len(orders)
+    states = []
+    for number in range(len(orders)):
+        part = partial[:, number * wide : (number + 1) * wide]
+        shape = (2,) * bits + (narrow_count, share_rows, wide)
+        states.append((part.reshape(shape), list(range(bits - 1, -1, -1)) + ["narrow"]))
+    for step in range(bits + 1):
+        for number, order in enumerate(orders):
+            held, axes = states[number]
+            axis = axes.index(order[step])
+            if order[step] == "narrow":
+                pieces = exchange(
+                    lambda peer: lax.dynamic_index_in_dim(held, peer, axis, False),
+                    narrow_count, narrow_index, "narrow",
+                )
+                held = jnp.sum(pieces.astype(jnp.float32), axis=0).astype(jnp.bfloat16)
+            else:
+                bit = order[step]
+                mine = lax.rem(lax.div(sec_index, 1 << bit), 2)
+                arrived = swap_bit(
+                    lax.dynamic_index_in_dim(held, 1 - mine, axis, False), bit, sec_count
+                )
+                kept = lax.dynamic_index_in_dim(held, mine, axis, False)
+                held = (kept.astype(jnp.float32) + arrived.astype(jnp.float32)).astype(jnp.bfloat16)
+            states[number] = (held, axes[:axis] + axes[axis + 1 :])
+    return jnp.concatenate([held for held, _ in states], axis=1)
+
+
+def reduce_orders(sec_count):
+    bits = list(range(sec_count.bit_length() - 1))
+    first, rest = bits[:1], bits[1:]
+    return (
+        first + ["narrow"] + rest,
+        first + rest + ["narrow"],
+    )
+
+
 def on_device(
     tokens, attn_gain, w_query, w_key, w_value, query_gain, key_gain, w_out, moe_gain,
     expert_ids, expert_weights, w_gate, w_up, w_down,
@@ -284,7 +331,7 @@
     mixture = experts_local(
         moe_all, ids, gates, (block_rows, slots), w_gate, w_up, w_down, sec_index * expert_here
     )
-    mixture = lax.psum_scatter(mixture, ("sec", "narrow"), scatter_dimension=0, tiled=True)
+    mixture = halves_reduce(mixture, reduce_orders(sec_count), share_rows)
     return (carried.astype(jnp.float32) + mixture.astype(jnp.float32)).astype(jnp.bfloat16)
 
 

time: 404 us -> 300 us (0.74)
  the two profiles are of different devices: /device:TPU:13 before, /device:TPU:0 now
where the time goes in v2:
time: 300 us
  waiting for transfers between devices  137 us (46%)
  Pallas kernels  48.8 us (16%)
  blocking collectives  30.5 us (10%)
  local copies, waits for them, and re-layouts  23.1 us (8%)
  other arithmetic  19.9 us (7%)
  starting transfers between devices  14.7 us (5%)
  between operations  14.1 us (5%)
  matrix products  11.5 us (4%)
    all_gather x1, waiting for transfers between devices, on_device(): moe_all = lax.all_gather(moe_in, ('sec', 'narrow'), axis=0, tiled=True)  49.4 us
    pallas_call x1, Pallas kernels, experts_local(): pl.pallas_call(experts_kernel, grid=(experts,), in_specs=[whole(x.shape),...  41.1 us
    ppermute x8, waiting for transfers between devices, swap_bit(): return lax.ppermute(piece, 'sec', [(i, i ^ 1 << bit) for i in range(count)])  39.6 us
    all_gather x1, waiting for transfers between devices, on_device(): keys_values = lax.all_gather(keys_values, 'sec', axis=0, tiled=True)  35.2 us
    all_gather x1, blocking collectives, on_device(): lax.all_gather(jnp.concatenate([expert_ids.astype(jnp.float32), gates_own...  30.5 us
    ppermute x4, waiting for transfers between devices, exchange(): lax.ppermute(pieces_for(target), axis, [(i, (i + shift) % count) for i in...  12.8 us
    convert_element_type x8, other arithmetic, halves_reduce(): (kept.astype(jnp.float32) + arrived.astype(jnp.float32)).astype(jnp.bfloa...  8.5 us
    ppermute x8, starting transfers between devices, swap_bit(): return lax.ppermute(piece, 'sec', [(i, i ^ 1 << bit) for i in range(count)])  8.09 us
  transfers between devices with their start and end apart: 14, of which 13 were waited for; matrix products, arithmetic and copies ran while one was open for 12% of the time, Pallas kernels for 0%

profile of v2, /device:TPU:0, one launch (start us, length us, event | category | flops | bytes accessed | tf_op | source)
XLA Modules:
  0.0 299.6 jit_solution(12779316196118878422)
XLA Ops:
  10.7 3.0 %collective-permute-start = (f32[128,2,128]{0,2,1:T(8,128)S(1)}, f32[128,2,128]{0,2,1:T(8,128)S(1)}, u32[]{:S(2)}, u32[]{:S(2)}) collective-permute-start(f32[128,2,128]{0,2,1:T(8,128)S(1)} %copy.67), channel_id=1, source_target_pairs={{0,1},{1,0},{2,3},{3,2},{4,5},{5,4},{6,7},{7,6},{8,9},{9,8},{10,11... | collective-permute-start | bytes 393224 | tf_op jit(solution)/shard_map/ppermute | solution.py:198
  14.1 3.1 %collective-permute-done = f32[128,2,128]{0,2,1:T(8,128)S(1)} collective-permute-done((f32[128,2,128]{0,2,1:T(8,128)S(1)}, f32[128,2,128]{0,2,1:T(8,128)S(1)}, u32[]{:S(2)}, u32[]{:S(2)}) %collective-permute-start) | collective-permute-done | bytes 131104 | tf_op jit(solution)/shard_map/ppermute | solution.py:198
  18.5 4.7 %convolution_bitcast_fusion = f32[16,8,16,128]{3,1,2,0:T(8,128)S(1)} fusion(bf16[2048,2048]{1,0:T(8,128)(2,1)} %param.16, bf16[128,2048]{1,0:T(8,128)(2,1)S(1)} %copy-done.7, f32[2048]{0:T(1024)S(1)} %copy-done.9, f32[128]{0:T(128)S(1)} %add_rsqrt_fusion.3), kind=kOutput, calls=%fused_computation.22 | convolution fusion | flops 1074790400 | bytes 9970176 | tf_op jit(solution)/shard_map/dot_general | solution.py:306
  26.0 35.2 %all-gather.3.cloned.1.call-done.k_ref.v_ref = bf16[2048,512]{1,0:T(8,128)(2,1)} async-done(((bf16[128,512]{1,0:T(8,128)(2,1)}), bf16[2048,512]{1,0:T(8,128)(2,1)}) %all-gather.3.cloned.1.call-update) | async-done | bytes 2097168 | tf_op jit(solution)/shard_map/all_gather | solution.py:298
  61.3 7.8 %shard_map.136 = bf16[2048,128]{1,0:T(8,128)(2,1)} custom-call(bf16[2048,128]{1,0:T(8,128)(2,1)} %bitcast.129, bf16[2048,512]{1,0:T(8,128)(2,1)} %all-gather.3.cloned.1.call-done.k_ref.v_ref, bf16[2048,512]{1,0:T(8,128)(2,1)} %all-gather.3.cloned.1.call-done.k_ref.v_ref), custom_call_target="tpu_custom_call" | custom-call | tf_op jit(solution)/shard_map/pallas_call | solution.py:97
  70.4 4.7 %convolution_convert_fusion.2 = bf16[128,2048]{1,0:T(8,128)(2,1)S(1)} fusion(bf16[128,2048]{0,1:T(8,128)(2,1)S(1)} %bitcast.128, bf16[2048,2048]{1,0:T(8,128)(2,1)} %param.21), kind=kOutput, calls=%fused_computation.13 | convolution fusion | flops 1074003968 | bytes 9437184 | tf_op jit(solution)/shard_map/dot_general | solution.py:317
  76.7 6.9 %collective-permute-done.1 = bf16[64,2048]{1,0:T(8,128)(2,1)S(1)} collective-permute-done((bf16[64,2048]{1,0:T(8,128)(2,1)S(1)}, bf16[64,2048]{1,0:T(8,128)(2,1)S(1)}, u32[]{:S(2)}, u32[]{:S(2)}) %collective-permute-start.1) | collective-permute-done | bytes 262176 | tf_op jit(solution)/shard_map/ppermute | solution.py:198
  84.9 30.5 %all_gather.11 = f32[2048,16]{0,1:T(8,128)S(1)} all-gather(f32[128,16]{0,1:T(8,128)S(1)} %pad_maximum_fusion.1), channel_id=1, replica_groups=mesh['sec'=16,'narrow'=2] {'sec'}, dimensions={0}, use_global_device_ids=true | all-gather | bytes 139264 | tf_op jit(solution)/shard_map/all_gather | solution.py:299
  116.5 1.7 reshape.209.weight_ref
  118.2 1.5 fusion.3.pick_ref
  119.7 2.6 fusion.2.back_ref
  122.3 49.4 %all-gather.5.cloned.1.call-done.x_ref = bf16[2048,2048]{1,0:T(8,128)(2,1)} async-done(((bf16[64,2048]{1,0:T(8,128)(2,1)}), bf16[2048,2048]{1,0:T(8,128)(2,1)}) %all-gather.5.cloned.1.call-update) | async-done | bytes 8388624 | tf_op jit(solution)/shard_map/all_gather | solution.py:326
  171.7 41.1 %shard_map.137 = bf16[2048,2048]{1,0:T(8,128)(2,1)} custom-call(bf16[2048,2048]{1,0:T(8,128)(2,1)} %all-gather.5.cloned.1.call-done.x_ref, bf16[4,8,80,256]{3,2,1,0:T(8,128)(2,1)} %fusion.3.pick_ref, bf16[4,8,256,80]{3,2,1,0:T(8,128)(2,1)} %fusion.2.back_ref, f32[4,640,1]{2,1,0:T(8,128)} %reshape.209.weight_ref, bf16[4,2048,384]{2,1,0:T(8,128)(2,1)} %gate_ref.1, ...), custom_call_target="tpu_custom_call" | custom-call | tf_op jit(solution)/shard_map/pallas_call | solution.py:169
  212.8 4.1 %fusion.41 = (bf16[2048,1024]{1,0:T(8,128)(2,1)S(1)}, bf16[2048,1024]{1,0:T(8,128)(2,1)S(1)}) fusion(bf16[2048,2048]{1,0:T(8,128)(2,1)} %shard_map.137), kind=kLoop, calls=%fused_computation.118 | loop fusion | bytes 16777216 | tf_op jit(solution)/shard_map/slice | solution.py:218
  216.9 1.8 dynamic-slice_bitcast_fusion
  219.0 2.1 dynamic-slice_bitcast_fusion.1
  223.1 2.7 fusion
  225.9 1.5 collective-permute-start.8
  227.5 2.6 fusion.1
  231.7 1.6 broadcast_in_dim.56
  234.4 17.0 %collective-permute-done.8 = bf16[2,2,2,64,1024]{4,3,2,1,0:T(8,128)(2,1)} collective-permute-done((bf16[2,2,2,64,1024]{4,3,2,1,0:T(8,128)(2,1)S(1)}, bf16[2,2,2,64,1024]{4,3,2,1,0:T(8,128)(2,1)}, u32[]{:S(2)}, u32[]{:S(2)}) %collective-permute-start.8) | collective-permute-done | bytes 1048608 | tf_op jit(solution)/shard_map/ppermute | solution.py:206
  251.4 1.6 fusion.10
  256.5 2.3 bitcast_dynamic-update-slice_fusion
  258.9 2.2 reduce_sum.104
  262.1 5.4 %collective-permute-done.9 = bf16[2,2,64,1024]{3,2,1,0:T(8,128)(2,1)} collective-permute-done((bf16[2,2,64,1024]{3,2,1,0:T(8,128)(2,1)}, bf16[2,2,64,1024]{3,2,1,0:T(8,128)(2,1)}, u32[]{:S(2)}, u32[]{:S(2)}) %collective-permute-start.9) | collective-permute-done | bytes 524320 | tf_op jit(solution)/shard_map/ppermute | solution.py:206
  268.8 2.0 collective-permute-start.10
  270.8 3.5 %collective-permute-done.4 = bf16[2,2,64,1024]{3,2,0,1:T(8,128)(2,1)S(1)} collective-permute-done((bf16[2,2,64,1024]{3,2,0,1:T(8,128)(2,1)S(1)}, bf16[2,2,64,1024]{3,2,0,1:T(8,128)(2,1)S(1)}, u32[]{:S(2)}, u32[]{:S(2)}) %collective-permute-start.4) | collective-permute-done | bytes 524320 | tf_op jit(solution)/shard_map/ppermute | solution.py:206
  274.5 1.6 collective-permute-start.5
  276.0 6.2 %collective-permute-done.10 = bf16[2,64,1024]{2,1,0:T(8,128)(2,1)S(1)} collective-permute-done((bf16[2,64,1024]{2,1,0:T(8,128)(2,1)S(1)}, bf16[2,64,1024]{2,1,0:T(8,128)(2,1)S(1)}, u32[]{:S(2)}, u32[]{:S(2)}) %collective-permute-start.10) | collective-permute-done | bytes 262176 | tf_op jit(solution)/shard_map/ppermute | solution.py:206
  283.8 1.7 collective-permute-done.5
  285.7 1.7 collective-permute-done.11
  287.5 4.5 %collective-permute-done.6 = bf16[64,1024]{1,0:T(8,128)(2,1)S(1)} collective-permute-done((bf16[64,1024]{1,0:T(8,128)(2,1)S(1)}, bf16[64,1024]{1,0:T(8,128)(2,1)S(1)}, u32[]{:S(2)}, u32[]{:S(2)}) %collective-permute-start.6) | collective-permute-done | bytes 131104 | tf_op jit(solution)/shard_map/ppermute | solution.py:206
  (119 shorter events, 27.3 us)
Async XLA Ops:
  6.5 1.2 copy-start
  6.5 1.8 copy-start.8
  6.5 2.4 copy-start.7
  6.5 2.6 copy-start.9
  6.5 54.7 %all-gather.3.cloned.1.call-start = ((), (), s32[]{:S(2)}) async-start(), calls=%async_computation | async-start | bytes 2228224 | tf_op jit(solution)/shard_map/all_gather | solution.py:298
  10.0 7.3 %copy-start.13 = (f32[128]{0:T(128)S(1)}, f32[128]{0:T(128)}, u32[]{:S(2)}) copy-start(f32[128]{0:T(128)} %param.20) | copy-start | bytes 1540
  10.7 6.5 %collective-permute-start = (f32[128,2,128]{0,2,1:T(8,128)S(1)}, f32[128,2,128]{0,2,1:T(8,128)S(1)}, u32[]{:S(2)}, u32[]{:S(2)}) collective-permute-start(f32[128,2,128]{0,2,1:T(8,128)S(1)} %copy.67), channel_id=1, source_target_pairs={{0,1},{1,0},{2,3},{3,2},{4,5},{5,4},{6,7},{7,6},{8,9},{9,8},{10,11... | collective-permute-start | bytes 393224 | tf_op jit(solution)/shard_map/ppermute | solution.py:198
  18.2 153.5 %all-gather.5.cloned.1.call-start = ((), (), s32[]{:S(2)}) async-start(), calls=%async_computation.1 | async-start | bytes 8650752 | tf_op jit(solution)/shard_map/all_gather | solution.py:326
  23.1 0.7 copy-start.14
  75.0 8.9 %copy-start.11 = (f32[2048]{0:T(1024)S(1)}, f32[2048]{0:T(1024)}, u32[]{:S(2)}) copy-start(f32[2048]{0:T(1024)} %param.22) | copy-start | bytes 24580
  75.0 9.8 %copy-start.10 = (f32[128,8]{0,1:T(8,128)S(1)}, f32[128,8]{0,1:T(8,128)}, u32[]{:S(2)}) copy-start(f32[128,8]{0,1:T(8,128)} %param.24) | copy-start | bytes 12292
  75.1 9.8 %copy-start.12 = (s32[128,8]{0,1:T(8,128)S(1)}, s32[128,8]{0,1:T(8,128)}, u32[]{:S(2)}) copy-start(s32[128,8]{0,1:T(8,128)} %param.23) | copy-start | bytes 12292
  75.1 8.5 %collective-permute-start.1 = (bf16[64,2048]{1,0:T(8,128)(2,1)S(1)}, bf16[64,2048]{1,0:T(8,128)(2,1)S(1)}, u32[]{:S(2)}, u32[]{:S(2)}) collective-permute-start(bf16[64,2048]{1,0:T(8,128)(2,1)S(1)} %constant_dynamic-slice_fusion.2), channel_id=1, source_target_pairs={{0,1},{1,0},{2,3},{3,2},{4,5},{5,4},{6,7},{7,6},{8,9},{9,8},{10,11... | collective-permute-start | bytes 786440 | tf_op jit(solution)/shard_map/ppermute | solution.py:198
  216.9 4.2 %copy-start.2 = (bf16[2048,1024]{1,0:T(8,128)(2,1)}, bf16[2048,1024]{1,0:T(8,128)(2,1)S(1)}, u32[]{:S(2)}) copy-start(bf16[2048,1024]{1,0:T(8,128)(2,1)S(1)} %get-tuple-element.7) | copy-start | bytes 12582916
  216.9 4.5 %copy-start.4 = (bf16[2048,1024]{1,0:T(8,128)(2,1)}, bf16[2048,1024]{1,0:T(8,128)(2,1)S(1)}, u32[]{:S(2)}) copy-start(bf16[2048,1024]{1,0:T(8,128)(2,1)S(1)} %get-tuple-element.8) | copy-start | bytes 12582916
  218.7 4.4 %collective-permute-start.7 = (bf16[2,2,2,2,64,1024]{5,4,3,2,1,0:T(8,128)(2,1)}, bf16[2,2,2,2,64,1024]{5,4,3,2,1,0:T(8,128)(2,1)S(1)}, u32[]{:S(2)}, u32[]{:S(2)}) collective-permute-start(bf16[2,2,2,2,64,1024]{5,4,3,2,1,0:T(8,128)(2,1)} %dynamic-slice_bitcast_fusion), channel_id=1, source_target_pairs={{0,2},{2,0},{4,6},{6,4},{8,10},{10,8},{12,14},{14,12},{16,18},{18,... | collective-permute-start | bytes 6291464 | tf_op jit(solution)/shard_map/ppermute | solution.py:206
  221.5 6.0 %collective-permute-start.2 = (bf16[2,2,2,2,64,1024]{5,4,3,2,1,0:T(8,128)(2,1)}, bf16[2,2,2,2,64,1024]{5,4,3,2,1,0:T(8,128)(2,1)}, u32[]{:S(2)}, u32[]{:S(2)}) collective-permute-start(bf16[2,2,2,2,64,1024]{5,4,3,2,1,0:T(8,128)(2,1)} %dynamic-slice_bitcast_fusion.1), channel_id=1, source_target_pairs={{0,2},{2,0},{4,6},{6,4},{8,10},{10,8},{12,14},{14,12},{16,18},{18,... | collective-permute-start | bytes 6291464 | tf_op jit(solution)/shard_map/ppermute | solution.py:206
  223.1 4.4 %copy-start.3 = (bf16[2048,1024]{1,0:T(8,128)(2,1)S(1)}, bf16[2048,1024]{1,0:T(8,128)(2,1)}, u32[]{:S(2)}) copy-start(bf16[2048,1024]{1,0:T(8,128)(2,1)} %copy-done.2) | copy-start | bytes 12582916
  225.8 4.3 %copy-start.5 = (bf16[2,2,2,2,64,1024]{5,4,3,2,1,0:T(8,128)(2,1)}, bf16[2,2,2,2,64,1024]{5,4,3,2,1,0:T(8,128)(2,1)S(1)}, u32[]{:S(2)}) copy-start(bf16[2,2,2,2,64,1024]{5,4,3,2,1,0:T(8,128)(2,1)S(1)} %fusion) | copy-start | bytes 6291460
  225.9 25.5 %collective-permute-start.8 = (bf16[2,2,2,64,1024]{4,3,2,1,0:T(8,128)(2,1)S(1)}, bf16[2,2,2,64,1024]{4,3,2,1,0:T(8,128)(2,1)}, u32[]{:S(2)}, u32[]{:S(2)}) collective-permute-start(bf16[2,2,2,64,1024]{4,3,2,1,0:T(8,128)(2,1)S(1)} %dynamic-slice_bitcast_fusion.2), channel_id=1, source_target_pairs={{0,4},{2,6},{4,0},{6,2},{8,12},{10,14},{12,8},{14,10},{16,20},{18,... | collective-permute-start | bytes 3145736 | tf_op jit(solution)/shard_map/ppermute | solution.py:206
  231.2 25.4 %collective-permute-start.3 = (bf16[2,2,2,64,1024]{4,3,2,1,0:T(8,128)(2,1)}, bf16[2,2,2,64,1024]{4,3,2,1,0:T(8,128)(2,1)}, u32[]{:S(2)}, u32[]{:S(2)}) collective-permute-start(bf16[2,2,2,64,1024]{4,3,2,1,0:T(8,128)(2,1)} %dynamic-slice_bitcast_fusion.3), channel_id=1, source_target_pairs={{0,1},{1,0},{2,3},{3,2},{4,5},{5,4},{6,7},{7,6},{8,9},{9,8},{10,11... | collective-permute-start | bytes 3145736 | tf_op jit(solution)/shard_map/ppermute | solution.py:198
  231.7 19.7 %copy-start.6 = (bf16[2,2,2,2,64,1024]{5,4,3,2,1,0:T(8,128)(2,1)S(1)}, bf16[2,2,2,2,64,1024]{5,4,3,2,1,0:T(8,128)(2,1)}, u32[]{:S(2)}) copy-start(bf16[2,2,2,2,64,1024]{5,4,3,2,1,0:T(8,128)(2,1)} %copy-done.5) | copy-start | bytes 6291460
  253.9 13.6 %collective-permute-start.9 = (bf16[2,2,64,1024]{3,2,1,0:T(8,128)(2,1)}, bf16[2,2,64,1024]{3,2,1,0:T(8,128)(2,1)}, u32[]{:S(2)}, u32[]{:S(2)}) collective-permute-start(bf16[2,2,64,1024]{3,2,1,0:T(8,128)(2,1)} %dynamic-slice_bitcast_fusion.4), channel_id=1, source_target_pairs={{0,8},{2,10},{4,12},{6,14},{8,0},{10,2},{12,4},{14,6},{16,24},{18,... | collective-permute-start | bytes 1572872 | tf_op jit(solution)/shard_map/ppermute | solution.py:206
  261.2 13.0 %collective-permute-start.4 = (bf16[2,2,64,1024]{3,2,0,1:T(8,128)(2,1)S(1)}, bf16[2,2,64,1024]{3,2,0,1:T(8,128)(2,1)S(1)}, u32[]{:S(2)}, u32[]{:S(2)}) collective-permute-start(bf16[2,2,64,1024]{3,2,0,1:T(8,128)(2,1)S(1)} %bitcast.135), channel_id=1, source_target_pairs={{0,4},{2,6},{4,0},{6,2},{8,12},{10,14},{12,8},{14,10},{16,20},{18,... | collective-permute-start | bytes 1572872 | tf_op jit(solution)/shard_map/ppermute | solution.py:206
  268.8 13.4 %collective-permute-start.10 = (bf16[2,64,1024]{2,1,0:T(8,128)(2,1)S(1)}, bf16[2,64,1024]{2,1,0:T(8,128)(2,1)S(1)}, u32[]{:S(2)}, u32[]{:S(2)}) collective-permute-start(bf16[2,64,1024]{2,1,0:T(8,128)(2,1)S(1)} %dynamic-slice_bitcast_fusion.5), channel_id=1, source_target_pairs={{0,16},{2,18},{4,20},{6,22},{8,24},{10,26},{12,28},{14,30},{16,0},... | collective-permute-start | bytes 786440 | tf_op jit(solution)/shard_map/ppermute | solution.py:206
  274.2 18.5 %copy-start.1 = (bf16[2048,256]{1,0:T(8,128)(2,1)S(1)}, bf16[2048,256]{1,0:T(8,128)(2,1)}, u32[]{:S(2)}) copy-start(bf16[2048,256]{1,0:T(8,128)(2,1)} %param.17) | copy-start | bytes 3145732
  274.5 11.0 %collective-permute-start.5 = (bf16[2,64,1024]{2,1,0:T(8,128)(2,1)S(1)}, bf16[2,64,1024]{2,1,0:T(8,128)(2,1)S(1)}, u32[]{:S(2)}, u32[]{:S(2)}) collective-permute-start(bf16[2,64,1024]{2,1,0:T(8,128)(2,1)S(1)} %dynamic-slice_bitcast_fusion.6), channel_id=1, source_target_pairs={{0,8},{2,10},{4,12},{6,14},{8,0},{10,2},{12,4},{14,6},{16,24},{18,... | collective-permute-start | bytes 786440 | tf_op jit(solution)/shard_map/ppermute | solution.py:206
  282.4 5.0 %collective-permute-start.11 = (bf16[64,1024]{1,0:T(8,128)(2,1)S(1)}, bf16[64,1024]{1,0:T(8,128)(2,1)S(1)}, u32[]{:S(2)}, u32[]{:S(2)}) collective-permute-start(bf16[64,1024]{1,0:T(8,128)(2,1)S(1)} %get-tuple-element.13), channel_id=1, source_target_pairs={{0,1},{1,0},{2,3},{3,2},{4,5},{5,4},{6,7},{7,6},{8,9},{9,8},{10,11... | collective-permute-start | bytes 393224 | tf_op jit(solution)/shard_map/ppermute | solution.py:198
  285.6 6.3 %collective-permute-start.6 = (bf16[64,1024]{1,0:T(8,128)(2,1)S(1)}, bf16[64,1024]{1,0:T(8,128)(2,1)S(1)}, u32[]{:S(2)}, u32[]{:S(2)}) collective-permute-start(bf16[64,1024]{1,0:T(8,128)(2,1)S(1)} %dynamic-slice_bitcast_fusion.8), channel_id=1, source_target_pairs={{0,16},{2,18},{4,20},{6,22},{8,24},{10,26},{12,28},{14,30},{16,0},... | collective-permute-start | bytes 393224 | tf_op jit(solution)/shard_map/ppermute | solution.py:206
Sparse Core Ops, SparseCore 0:
  18.3 42.8 all-gather.2
  84.9 86.7 all-gather.4
